TPU v7x, 32 devices: a whole 2x2x4 slice. The times are simulated.
32 devices in a mesh: patch: 16 (over z, x, core), normal: 2 (over y).
Axes of the slice: x: 2, y: 2, z: 4, core: 2. Of those that a mesh axis runs over, the one named last changes fastest.
Arguments:
- residual_in: float32 [5, 128, 4096], P(None, 'normal', 'patch'), may hold values from -1.5 to 1.5
- prior_iterate: float32 [5, 128, 4096], P(None, 'normal', 'patch'), may hold values from -1.5 to 1.5
- coupling: float32 [4, 4096], P(None, 'patch'), may hold values from 0.2 to 0.6
- line_slot: int32 [4, 4096], P(None, 'patch'), may hold values from 0 to 127
- patch_nbr: int32 [16, 4], P('patch'), may hold values from 0 to 15, as said below
- edge_lines: int32 [16, 128], P('patch'), may hold values from 0 to 255, as said below
- upper_blocks: float32 [5, 5, 128, 4096], P(None, None, 'normal', 'patch'), may hold values from -1 to 1
- lower_blocks: float32 [5, 5, 128, 4096], P(None, None, 'normal', 'patch'), may hold values from -1 to 1
Outputs:
- adjoint: float32 [5, 128, 4096], P(None, 'normal', 'patch')
Inputs may be any that keep to these rules, and one draw needn't show every extreme that they name: `patch_nbr`: each neighbour slot of patch p names a patch at cyclic distance 1 or 2 from p in patch order; slots may repeat. `edge_lines`: the 128 entries of a row are distinct.
All inputs are finite; a program needn't handle non-finite values.
Results may differ from a plain program's by a relative error of at most 0.0001.
Values sent between devices are 32-bit elements; how exact they have to be, the bound alone decides.
A program may use at most 64 MiB of HBM per device.

v0:
```python
import jax
import jax.numpy as jnp
from jax import lax
from jax.sharding import PartitionSpec as P


def carried_in(part, axis, combine, identity, reverse):
    count = lax.axis_size(axis)
    place = lax.axis_index(axis)
    ahead = count - 1 - place if reverse else place
    gathered = jax.tree.map(lambda a: lax.all_gather(a, axis), part)
    state = jax.tree.map(lambda a, e: jnp.zeros_like(a) + jnp.asarray(e, a.dtype), part, identity)

    def one(step, state):
        source = count - 1 - step if reverse else step
        return combine(
            state, jax.tree.map(lambda a: lax.dynamic_index_in_dim(a, source, 0, False), gathered)
        )

    return lax.fori_loop(0, ahead, one, state)


def with_halo(value, sides, width):
    for axis, dim in sides:
        count, length = (lax.axis_size(axis), value.shape[dim])
        up = [(i, (i + 1) % count) for i in range(count)]
        down = [(j, i) for i, j in up]
        last = lax.slice_in_dim(value, length - width, length, axis=dim)
        initial = lax.slice_in_dim(value, 0, width, axis=dim)
        before = lax.ppermute(last, axis, up)
        after = lax.ppermute(initial, axis, down)
        value = jnp.concatenate([before, value, after], axis=dim)
    return value


def compose(first_map, second_map):
    first_mat, first_col = first_map
    second_mat, second_col = second_map
    count = first_mat.shape[0]
    joined_mat = second_mat[:, 0][:, None] * first_mat[0][None]
    joined_col = second_mat[:, 0][:, None] * first_col[0][None]
    for inner in range(1, count):
        joined_mat = joined_mat + second_mat[:, inner][:, None] * first_mat[inner][None]
        joined_col = joined_col + second_mat[:, inner][:, None] * first_col[inner][None]
    return (joined_mat, joined_col + second_col)


def inbound_state(device_map, identity, reverse):
    if reverse:
        return carried_in(device_map, "normal", compose, identity, True)
    return carried_in(device_map, "normal", compose, identity, False)


def to_blocks(array_in, block_lines):
    shape_in = array_in.shape
    split = array_in.reshape(shape_in[:-1] + (shape_in[-1] // block_lines, block_lines))
    return jnp.moveaxis(split, -2, 0)


def from_blocks(array_in):
    joined = jnp.moveaxis(array_in, 0, -2)
    return joined.reshape(joined.shape[:-2] + (joined.shape[-2] * joined.shape[-1],))


def line_sweep(blocks, forcing, reverse):
    variables = forcing.shape[0]
    width = forcing.shape[2]
    block_lines = 128
    step_maps = -jnp.swapaxes(blocks, 0, 1)
    column = forcing[:, None]
    if reverse:
        step_maps = jnp.flip(step_maps, 2)
        column = jnp.flip(column, 2)
    maps_blocked = to_blocks(step_maps, block_lines)
    cols_blocked = to_blocks(column, block_lines)

    def device_part(inputs):
        mats_here, cols_here = inputs
        prefix_mats, prefix_cols = lax.associative_scan(compose, (mats_here, cols_here), axis=2)
        return (prefix_mats[:, :, -1], prefix_cols[:, :, -1])

    end_mats, end_cols = lax.map(device_part, (maps_blocked, cols_blocked))
    device_map = (from_blocks(end_mats), from_blocks(end_cols))
    eye_part = jnp.broadcast_to(
        jnp.eye(variables, dtype=jnp.float32)[:, :, None], (variables, variables, width)
    )
    identity = (eye_part, jnp.zeros((variables, 1, width), jnp.float32))
    incoming = inbound_state(device_map, identity, reverse)
    incoming_blocked = to_blocks(incoming[1], block_lines)

    def apply_part(inputs):
        mats_here, cols_here, state_in = inputs
        prefix_mats, prefix_cols = lax.associative_scan(compose, (mats_here, cols_here), axis=2)
        total = prefix_cols[:, 0]
        for inner in range(variables):
            total = total + prefix_mats[:, inner] * state_in[inner, 0][None, None]
        return total

    result = from_blocks(lax.map(apply_part, (maps_blocked, cols_blocked, incoming_blocked)))
    if reverse:
        result = jnp.flip(result, 1)
    return result


def local(
    residual_in,
    prior_iterate,
    coupling,
    line_slot,
    patch_nbr,
    edge_lines,
    upper_blocks,
    lower_blocks,
):
    exported = jnp.take(prior_iterate, edge_lines[0], axis=2)
    own_patch = lax.axis_index("patch")
    patches_all = lax.axis_size("patch")
    relative = (patch_nbr[0] - own_patch + patches_all) % patches_all
    table = jnp.array([patches_all - 2, patches_all - 1, 1, 2], jnp.int32)
    nearby = with_halo(exported[None], (("patch", 0),), 1)
    forward = jnp.stack([nearby[2], nearby[0]], axis=0)
    further = with_halo(forward, (("patch", 0),), 1)
    stacked = jnp.stack([further[0], nearby[0], nearby[2], further[3]], axis=0)
    position = jnp.sum(
        jnp.where(relative[:, None] == table[None, :], jnp.arange(4, dtype=jnp.int32)[None, :], 0),
        axis=1,
    )
    source = stacked[position]
    picked = jnp.take_along_axis(source, line_slot[:, None, None, :], axis=3)
    forcing = residual_in - jnp.sum(picked * coupling[:, None, None, :], axis=0)
    upward = line_sweep(upper_blocks, forcing, False)
    return line_sweep(lower_blocks, upward, True)


def solution(mesh):
    in_specs = (
        P(None, "normal", "patch"),
        P(None, "normal", "patch"),
        P(None, "patch"),
        P(None, "patch"),
        P("patch", None),
        P("patch", None),
        P(None, None, "normal", "patch"),
        P(None, None, "normal", "patch"),
    )
    out_specs = P(None, "normal", "patch")
    return jax.shard_map(local, mesh=mesh, in_specs=in_specs, out_specs=out_specs, check_vma=False)
```

profile of v0, /device:TPU:26, one launch (start us, length us, event | category | flops | bytes accessed | tf_op | source)
XLA Modules:
  0.0 207.4 jit_solution(11722505557203870735)
XLA Ops:
  4.6 1.7 collective-permute-start.2
  8.7 10.5 %collective-permute-done = f32[1,5,64,128]{2,1,3,0:T(8,128)} collective-permute-done((f32[1,5,64,128]{2,1,3,0:T(8,128)}, f32[1,5,64,128]{2,1,3,0:T(8,128)}, u32[]{:S(2)}, u32[]{:S(2)}) %collective-permute-start) | collective-permute-done | bytes 163872 | tf_op jit(solution)/shard_map/ppermute | solution.py:30
  19.2 4.6 %collective-permute-done.2 = f32[1,5,64,128]{2,1,3,0:T(8,128)} collective-permute-done((f32[1,5,64,128]{2,1,3,0:T(8,128)}, f32[1,5,64,128]{2,1,3,0:T(8,128)}, u32[]{:S(2)}, u32[]{:S(2)}) %collective-permute-start.2) | collective-permute-done | bytes 163872 | tf_op jit(solution)/shard_map/ppermute | solution.py:31
  23.7 1.9 collective-permute-start.3
  25.6 2.0 reshape.1240
  28.5 2.1 reshape.1241
  37.4 11.1 %gather_fusion.2 = f32[1024,5,64]{2,1,0:T(8,128)} fusion(f32[4,5,64,128]{2,1,3,0:T(8,128)S(1)} %copy.122, s32[1024]{0:T(1024)S(1)} %bitcast.2130), kind=kCustom, calls=%fused_computation.2 | custom fusion | bytes 2629632 | tf_op jit(solution)/shard_map/jit(take_along_axis)/gather | solution.py:129
  48.5 6.1 %multiply_reduce_fusion = f32[256,5,64]{2,1,0:T(8,128)S(1)} fusion(f32[4,256,5,64]{3,2,1,0:T(8,128)} %bitcast.2145, f32[4,256]{1,0:T(4,128)S(1)} %copy-done.10, pred[4,256]{1,0:T(4,128)(4,1)S(1)} %compare_and_fusion), kind=kLoop, calls=%fused_computation.907 | loop fusion | flops 901120 | bytes 1643520 | tf_op jit(solution)/shard_map/reduce_sum | solution.py:130
  55.2 35.0 %while.70 = (s32[]{:T(128)}, f32[2,5,5,128]{3,0,2,1:T(2,128)S(1)}, f32[2,5,1,128]{3,0,2,1:T(2,128)S(1)}, f32[2,5,5,64,128]{4,0,3,1,2:T(2,128)}, f32[2,5,1,64,128...) while((s32[]{:T(128)}, f32[2,5,5,128]{3,0,2,1:T(2,128)S(1)}, f32[2,5,1,128]{3,0,2,1:T(2,128)S(1)}, ...), condition=%wide.region_3.4_spmd, body=%wide.region_2.3_spmd.sunk | while | flops 3589762 | bytes 26286252 | solution.py:82
  55.3 2.3 %constant_dynamic-slice_fusion.12 = f32[1,5,5,64,128]{4,0,3,1,2:T(1,128)S(1)} fusion(f32[2,5,5,64,128]{4,0,3,1,2:T(2,128)} %get-tuple-element.2926, s32[]{:T(128)} %get-tuple-element.2915), kind=kLoop, calls=%fused_computation.190.clone.1 | loop fusion | bytes 1638404 | tf_op jit(solution)/shard_map/while/body/jit(dynamic_index_in_dim)/dynamic_slice | solution.py:82
  65.1 2.0 pad.1003
  71.1 1.5 pad.1000
  72.8 2.3 %constant_dynamic-slice_fusion.12 = f32[1,5,5,64,128]{4,0,3,1,2:T(1,128)S(1)} fusion(f32[2,5,5,64,128]{4,0,3,1,2:T(2,128)} %get-tuple-element.2926, s32[]{:T(128)} %get-tuple-element.2915), kind=kLoop, calls=%fused_computation.190.clone.1 | loop fusion | bytes 1638404 | tf_op jit(solution)/shard_map/while/body/jit(dynamic_index_in_dim)/dynamic_slice | solution.py:82
  82.6 2.0 pad.1003
  88.6 1.5 pad.1000
  90.3 4.7 %all_gather.12 = f32[2,5,5,256]{3,2,1,0:T(8,128)S(1)} all-gather(f32[1,5,5,256]{3,2,1,0:T(8,128)S(1)} %all_gather_reshape.12), channel_id=1, replica_groups=mesh['patch'=16,'normal'=2] {'normal'}, dimensions={0}, use_global_device_ids=true | all-gather | bytes 76800 | tf_op jit(solution)/shard_map/all_gather | solution.py:11
  95.0 4.3 %all_gather.13 = f32[2,5,1,256]{3,2,1,0:T(1,128)S(1)} all-gather(f32[1,5,1,256]{3,2,1,0:T(1,128)S(1)} %bitcast.2323), channel_id=1, replica_groups=mesh['patch'=16,'normal'=2] {'normal'}, dimensions={0}, use_global_device_ids=true | all-gather | bytes 15360 | tf_op jit(solution)/shard_map/all_gather | solution.py:11
  100.6 27.8 %while.72 = (s32[]{:T(128)}, f32[2,5,64,128]{3,2,1,0:T(8,128)}, f32[2,5,1,64,128]{4,3,1,2,0:T(8,128)S(1)}, f32[2,5,5,64,128]{4,0,3,1,2:T(2,128)}, f32[2,5,1,128]{3,0,2,1:T(2,128)}, /*index=5*/s32[]{:T(128)}, f32[]{:T(128)}) while((s32[]{:T(128)}, f32[2,5,64,128]{3,2,1,0:T(8,128)}, f32[2,5,1,64,128]{4,3,1,2,0:T(8,128)S(1)}, ...), condition=%wide.region_7.8_spmd, body=%wide.region_6.7_spmd.sunk | while | flops 5574402 | bytes 36308736 | solution.py:99
  100.7 2.3 %constant_dynamic-slice_fusion.14 = f32[1,5,5,64,128]{4,0,3,1,2:T(1,128)S(1)} fusion(f32[2,5,5,64,128]{4,0,3,1,2:T(2,128)} %get-tuple-element.2972, s32[]{:T(128)} %get-tuple-element.2962), kind=kLoop, calls=%fused_computation.429.clone.1 | loop fusion | bytes 1638404 | tf_op jit(solution)/shard_map/while/body/jit(dynamic_index_in_dim)/dynamic_slice | solution.py:82
  114.6 2.3 %constant_dynamic-slice_fusion.14 = f32[1,5,5,64,128]{4,0,3,1,2:T(1,128)S(1)} fusion(f32[2,5,5,64,128]{4,0,3,1,2:T(2,128)} %get-tuple-element.2972, s32[]{:T(128)} %get-tuple-element.2962), kind=kLoop, calls=%fused_computation.429.clone.1 | loop fusion | bytes 1638404 | tf_op jit(solution)/shard_map/while/body/jit(dynamic_index_in_dim)/dynamic_slice | solution.py:82
  130.3 35.0 %while.73 = (s32[]{:T(128)}, f32[2,5,5,128]{3,0,2,1:T(2,128)S(1)}, f32[2,5,1,128]{3,0,2,1:T(2,128)S(1)}, f32[2,5,5,64,128]{4,0,3,1,2:T(2,128)}, f32[2,5,1,64,128...) while((s32[]{:T(128)}, f32[2,5,5,128]{3,0,2,1:T(2,128)S(1)}, f32[2,5,1,128]{3,0,2,1:T(2,128)S(1)}, ...), condition=%wide.region_9.10_spmd, body=%wide.region_8.9_spmd.sunk | while | flops 3589762 | bytes 26286252 | solution.py:82
  130.4 2.3 %constant_dynamic-slice_fusion.15 = f32[1,5,5,64,128]{4,0,3,1,2:T(1,128)S(1)} fusion(f32[2,5,5,64,128]{4,0,3,1,2:T(2,128)} %get-tuple-element.2995, s32[]{:T(128)} %get-tuple-element.2984), kind=kLoop, calls=%fused_computation.642.clone.1 | loop fusion | bytes 1638404 | tf_op jit(solution)/shard_map/while/body/jit(dynamic_index_in_dim)/dynamic_slice | solution.py:82
  140.1 2.0 pad.1095
  146.1 1.5 pad.1092
  147.9 2.3 %constant_dynamic-slice_fusion.15 = f32[1,5,5,64,128]{4,0,3,1,2:T(1,128)S(1)} fusion(f32[2,5,5,64,128]{4,0,3,1,2:T(2,128)} %get-tuple-element.2995, s32[]{:T(128)} %get-tuple-element.2984), kind=kLoop, calls=%fused_computation.642.clone.1 | loop fusion | bytes 1638404 | tf_op jit(solution)/shard_map/while/body/jit(dynamic_index_in_dim)/dynamic_slice | solution.py:82
  157.6 2.0 pad.1095
  163.7 1.5 pad.1092
  165.3 5.6 %all_gather.14 = f32[2,5,5,256]{3,2,1,0:T(8,128)S(1)} all-gather(f32[1,5,5,256]{3,2,1,0:T(8,128)S(1)} %all_gather_reshape.14), channel_id=1, replica_groups=mesh['patch'=16,'normal'=2] {'normal'}, dimensions={0}, use_global_device_ids=true | all-gather | bytes 76800 | tf_op jit(solution)/shard_map/all_gather | solution.py:11
  170.9 4.3 %all_gather.15 = f32[2,5,1,256]{3,2,1,0:T(1,128)S(1)} all-gather(f32[1,5,1,256]{3,2,1,0:T(1,128)S(1)} %bitcast.2324), channel_id=1, replica_groups=mesh['patch'=16,'normal'=2] {'normal'}, dimensions={0}, use_global_device_ids=true | all-gather | bytes 15360 | tf_op jit(solution)/shard_map/all_gather | solution.py:11
  177.9 27.8 %while.75 = (s32[]{:T(128)}, f32[2,5,64,128]{3,2,1,0:T(8,128)}, f32[2,5,1,64,128]{4,3,1,2,0:T(8,128)S(1)}, f32[2,5,5,64,128]{4,0,3,1,2:T(2,128)}, f32[2,5,1,128]{3,0,2,1:T(2,128)}, /*index=5*/s32[]{:T(128)}, f32[]{:T(128)}) while((s32[]{:T(128)}, f32[2,5,64,128]{3,2,1,0:T(8,128)}, f32[2,5,1,64,128]{4,3,1,2,0:T(8,128)S(1)}, ...), condition=%wide.region_13.14_spmd, body=%wide.region_12.13_spmd.sunk | while | flops 5574402 | bytes 36308736 | solution.py:99
  177.9 2.3 %constant_dynamic-slice_fusion.17 = f32[1,5,5,64,128]{4,0,3,1,2:T(1,128)S(1)} fusion(f32[2,5,5,64,128]{4,0,3,1,2:T(2,128)} %get-tuple-element.3041, s32[]{:T(128)} %get-tuple-element.3031), kind=kLoop, calls=%fused_computation.881.clone.1 | loop fusion | bytes 1638404 | tf_op jit(solution)/shard_map/while/body/jit(dynamic_index_in_dim)/dynamic_slice | solution.py:82
  191.8 2.3 %constant_dynamic-slice_fusion.17 = f32[1,5,5,64,128]{4,0,3,1,2:T(1,128)S(1)} fusion(f32[2,5,5,64,128]{4,0,3,1,2:T(2,128)} %get-tuple-element.3041, s32[]{:T(128)} %get-tuple-element.3031), kind=kLoop, calls=%fused_computation.881.clone.1 | loop fusion | bytes 1638404 | tf_op jit(solution)/shard_map/while/body/jit(dynamic_index_in_dim)/dynamic_slice | solution.py:82
  (1199 shorter events, 109.5 us)
Async XLA Ops:
  0.0 6.4 %copy-start.9 = (s32[4,256]{1,0:T(4,128)S(1)}, s32[4,256]{1,0:T(4,128)}, u32[]{:S(2)}) copy-start(s32[4,256]{1,0:T(4,128)} %param.24) | copy-start | bytes 12292
  0.0 6.4 %copy-start.2 = (f32[5,5,64,256]{3,2,1,0:T(8,128)S(1)}, f32[5,5,64,256]{3,2,1,0:T(8,128)}, u32[]{:S(2)}) copy-start(f32[5,5,64,256]{3,2,1,0:T(8,128)} %param.27) | copy-start | bytes 4915204
  4.6 14.5 %collective-permute-start = (f32[1,5,64,128]{2,1,3,0:T(8,128)}, f32[1,5,64,128]{2,1,3,0:T(8,128)}, u32[]{:S(2)}, u32[]{:S(2)}) collective-permute-start(f32[1,5,64,128]{2,1,3,0:T(8,128)} %bitcast_select_fusion), channel_id=1, source_target_pairs={{0,2},{2,4},{4,6},{6,8},{8,10},{10,12},{12,14},{14,16},{16,18},{18... | collective-permute-start | bytes 491528 | tf_op jit(solution)/shard_map/ppermute | solution.py:30
  4.6 19.1 %collective-permute-start.2 = (f32[1,5,64,128]{2,1,3,0:T(8,128)}, f32[1,5,64,128]{2,1,3,0:T(8,128)}, u32[]{:S(2)}, u32[]{:S(2)}) collective-permute-start(f32[1,5,64,128]{2,1,3,0:T(8,128)} %bitcast_select_fusion), channel_id=1, source_target_pairs={{2,0},{4,2},{6,4},{8,6},{10,8},{12,10},{14,12},{16,14},{18,16},{20... | collective-permute-start | bytes 491528 | tf_op jit(solution)/shard_map/ppermute | solution.py:31
  6.4 1.4 copy-start.3
  7.8 0.7 copy-start.11
  7.8 0.7 copy-start.12
  19.2 14.4 %collective-permute-start.1 = (f32[1,5,64,128]{2,1,3,0:T(8,128)}, f32[1,5,64,128]{2,1,3,0:T(8,128)}, u32[]{:S(2)}, u32[]{:S(2)}) collective-permute-start(f32[1,5,64,128]{2,1,3,0:T(8,128)} %collective-permute-done), channel_id=1, source_target_pairs={{0,2},{2,4},{4,6},{6,8},{8,10},{10,12},{12,14},{14,16},{16,18},{18... | collective-permute-start | bytes 491528 | tf_op jit(solution)/shard_map/ppermute | solution.py:30
  23.7 11.1 %collective-permute-start.3 = (f32[1,5,64,128]{2,1,3,0:T(8,128)}, f32[1,5,64,128]{2,1,3,0:T(8,128)}, u32[]{:S(2)}, u32[]{:S(2)}) collective-permute-start(f32[1,5,64,128]{2,1,3,0:T(8,128)} %collective-permute-done.2), channel_id=1, source_target_pairs={{2,0},{4,2},{6,4},{8,6},{10,8},{12,10},{14,12},{16,14},{18,16},{20... | collective-permute-start | bytes 491528 | tf_op jit(solution)/shard_map/ppermute | solution.py:31
  37.4 11.1 %copy-start.10 = (f32[4,256]{1,0:T(4,128)S(1)}, f32[4,256]{1,0:T(4,128)}, u32[]{:S(2)}) copy-start(f32[4,256]{1,0:T(4,128)} %param.23) | copy-start | bytes 12292
  48.5 6.4 %copy-start.8 = (f32[5,64,256]{2,1,0:T(8,128)S(1)}, f32[5,64,256]{2,1,0:T(8,128)}, u32[]{:S(2)}) copy-start(f32[5,64,256]{2,1,0:T(8,128)} %param.21) | copy-start | bytes 983044
  109.8 0.9 copy-start
  112.5 1.2 copy-start.4
  113.8 0.7 copy-start.5
  123.6 0.9 copy-start
  126.4 1.2 copy-start.4
  127.7 0.7 copy-start.5
  187.0 0.9 copy-start.1
  189.7 1.2 copy-start.6
  191.0 0.7 copy-start.7
  200.9 0.9 copy-start.1
  203.6 1.2 copy-start.6
  204.9 0.7 copy-start.7
where the time goes:
time: 209 us; the launch traced here: 207 us
  local copies, waits for them, and re-layouts  128 us (61%)
  other arithmetic  34 us (16%)
  blocking collectives  18.9 us (9%)
  waiting for transfers between devices  15.7 us (8%)
  loops' own time  7.17 us (3%)
  starting transfers between devices  3.65 us (2%)
    pad x64, local copies, waits for them, and re-layouts, device_part(): lax.associative_scan(compose, (mats_here, cols_here), axis=2)  26.9 us
    dynamic_slice x16, local copies, waits for them, and re-layouts, line_sweep(): end_mats, end_cols = lax.map(device_part, (maps_blocked, cols_blocked))  20.7 us
    all_gather x4, blocking collectives, carried_in(): gathered = jax.tree.map(lambda a: lax.all_gather(a, axis), part)  18.9 us
    while x224, local copies, waits for them, and re-layouts  17.8 us
    pad x80, local copies, waits for them, and re-layouts, apply_part(): lax.associative_scan(compose, (mats_here, cols_here), axis=2)  12.4 us
    ppermute x2, waiting for transfers between devices, with_halo(): before = lax.ppermute(last, axis, up)  11.2 us
    gather x1, local copies, waits for them, and re-layouts, local(): picked = jnp.take_along_axis(source, line_slot[:, None, None, :], axis=3)  11.1 us
    slice x152, local copies, waits for them, and re-layouts, apply_part(): lax.associative_scan(compose, (mats_here, cols_here), axis=2)  10.5 us
  transfers between devices with their start and end apart: 4, of which 3 were waited for; matrix products, arithmetic and copies ran while one was open for 4% of the time, Pallas kernels for 0%

commit v1 on v0

v1 whole, which is shorter than its diff:
```python
import functools

import jax
import jax.numpy as jnp
from jax import lax
from jax.experimental import pallas as pl
from jax.experimental.pallas import tpu as pltpu
from jax.sharding import PartitionSpec as P

MESH = pl.DeviceIdType.MESH
CHUNK = 8
LANES = 128
F32 = jnp.float32
BF16 = jnp.bfloat16


def halves(x):
    high = x.astype(BF16)
    return high, (x - high.astype(F32)).astype(BF16)


def dot(a, b):
    return jnp.dot(a, b, preferred_element_type=F32)


def kernel(
    patches,
    count,
    prior_ref,
    coupling_ref,
    slot_ref,
    nbr_ref,
    edge_ref,
    residual_hbm,
    upper_hbm,
    lower_hbm,
    out_ref,
    residual,
    upper,
    lower,
    strip,
    halo,
    weight_hi,
    weight_lo,
    maps,
    force,
    up_state,
    up_out,
    up_in,
    down_out,
    down_in,
    local_sem,
    strip_send,
    strip_recv,
    line_send,
    line_recv,
):
    nv, cells, lines = prior_ref.shape
    slots = coupling_ref.shape[0]
    width = edge_ref.shape[1]
    seg = cells // CHUNK
    own = lax.axis_index("patch")
    place = lax.axis_index("normal")

    tiles = lines // LANES
    loads = [pltpu.make_async_copy(residual_hbm, residual, local_sem.at[2, 0])]
    for i, (src, dst) in enumerate(((upper_hbm, upper), (lower_hbm, lower))):
        for t in range(tiles):
            part = src.at[:, :, :, t * LANES : (t + 1) * LANES]
            loads.append(pltpu.make_async_copy(part, dst.at[t], local_sem.at[i, t]))
    for load in loads:
        load.start()

    core = lax.rem(own, 2)
    chip = lax.rem(own // 2, 2)
    core_mate = own + 1 - 2 * core
    chip_mate = own + 2 - 4 * chip
    ahead = lax.rem(own + 4 - 8 * chip + patches, patches)
    behind = lax.rem(own - 4 + 8 * chip + patches, patches)
    direct = 3 - 3 * chip

    barrier = pltpu.get_barrier_semaphore()
    for other in (core_mate, chip_mate, behind):
        pl.semaphore_signal(barrier, inc=1, device_id={"patch": other}, device_id_type=MESH)

    @pl.when(place > 0)
    def _():
        pl.semaphore_signal(barrier, inc=1, device_id={"normal": place - 1}, device_id_type=MESH)

    @pl.when(place < count - 1)
    def _():
        pl.semaphore_signal(barrier, inc=1, device_id={"normal": place + 1}, device_id_type=MESH)

    pick = jnp.where(
        lax.broadcasted_iota(jnp.int32, (lines, width), 0) == edge_ref[...], 1.0, 0.0
    ).astype(BF16)
    prior = prior_ref[...].reshape(nv * cells, lines)
    high = prior.astype(BF16)
    rest = prior - high.astype(F32)
    middle, low = halves(rest)
    exported = dot(high, pick) + (dot(middle, pick) + dot(low, pick))
    strip[...] = exported.reshape(nv, cells, width)

    below = (place + count - 1) // count
    above = (2 * count - 2 - place) // count
    pl.semaphore_wait(barrier, 3 + below + above)

    def send(kind, v, src, slot, other):
        return pltpu.make_async_remote_copy(
            src_ref=src,
            dst_ref=halo.at[slot, v],
            send_sem=strip_send.at[kind, v],
            recv_sem=strip_recv.at[kind, v],
            device_id={"patch": other},
            device_id_type=MESH,
        )

    to_chip = [send(0, v, strip.at[v], 3 - direct, chip_mate) for v in range(nv)]
    to_core = [send(1, v, strip.at[v], 1 + core, core_mate) for v in range(nv)]
    onward = [send(2, v, halo.at[direct, v], 3 - direct, ahead) for v in range(nv)]
    across = [send(3, v, halo.at[3 - 3 * core, v], 2 - core, core_mate) for v in range(nv)]
    for copy in to_chip + to_core:
        copy.start()

    row = lax.broadcasted_iota(jnp.int32, (width, lines), 0)
    offsets = (patches - 2, patches - 1, 1, 2)
    for s in range(4):
        total = jnp.zeros((width, lines), F32)
        for k in range(slots):
            relative = lax.rem(nbr_ref[0, k] - own + patches, patches)
            key = jnp.where(relative == offsets[s], slot_ref[k : k + 1, :], -1)
            total = total + jnp.where(row == key, coupling_ref[k : k + 1, :], 0.0)
        whi, wlo = halves(total)
        weight_hi[s * width : (s + 1) * width, :] = whi
        weight_lo[s * width : (s + 1) * width, :] = wlo

    def spread(ref, j, *at):
        parts = [ref[(t, *at, pl.ds(j, CHUNK, stride=seg))] for t in range(tiles)]
        return jnp.concatenate(parts, axis=1)

    def block(ref, w, v, j):
        return spread(ref, j, w, v)

    def advance(ref, j, state):
        result = []
        for v in range(nv):
            terms = [block(ref, w, v, j) * state[w] for w in range(nv)]
            result.append(((terms[0] + terms[1]) + (terms[2] + terms[3])) + terms[4])
        return result

    chunk_row = lax.broadcasted_iota(jnp.int32, (CHUNK, lines), 0)

    def shifted(x, by, reverse, fill):
        if reverse:
            return jnp.where(chunk_row < CHUNK - by, pltpu.roll(x, CHUNK - by, 0), fill)
        return jnp.where(chunk_row >= by, pltpu.roll(x, by, 0), fill)

    def map_column(ref, which, column, reverse):
        start = tuple(
            jnp.full((CHUNK, lines), 1.0 if v == column else 0.0, F32) for v in range(nv)
        )

        def one(step, state):
            j = seg - 1 - step if reverse else step
            return tuple(-x for x in advance(ref, j, state))

        end = lax.fori_loop(0, seg, one, start)
        for v in range(nv):
            maps[which, 0, v, column] = end[v]

    for load in loads:
        load.wait()
    for v in range(nv):
        to_chip[v].wait_recv()
        onward[v].start()
        map_column(upper, 0, v, False)
        map_column(lower, 1, v, True)

    def join(which, level, reverse):
        by = 1 << level
        for column in range(nv):
            prev = [
                shifted(maps[which, level, w, column], by, reverse, 1.0 if w == column else 0.0)
                for w in range(nv)
            ]
            for v in range(nv):
                total = maps[which, level, v, 0] * prev[0]
                for w in range(1, nv):
                    total = total + maps[which, level, v, w] * prev[w]
                maps[which, level + 1, v, column] = total

    for v in range(nv):
        onward[v].wait_recv()
        across[v].start()
        if v < 3:
            join(0, v, False)
            join(1, v, True)

    for v in range(nv):
        to_core[v].wait_recv()
        across[v].wait_recv()
    source = jnp.concatenate([halo[s].reshape(nv * cells, width) for s in range(4)], axis=1)
    source_hi, source_lo = halves(source)
    whole_hi = weight_hi[...]
    offline = dot(source_hi, whole_hi) + (dot(source_lo, whole_hi) + dot(source_hi, weight_lo[...]))
    forcing = residual[...] - offline.reshape(nv, cells, lines)
    for t in range(tiles):
        force[t] = forcing[:, :, t * LANES : (t + 1) * LANES]

    def read_force(v, j):
        return spread(force, j, v)

    def read_up(v, j):
        return up_state[v, j]

    def store_up(v, j, value):
        up_state[v, j] = value

    def store_out(v, j, value):
        for t in range(tiles):
            part = value[:, t * LANES : (t + 1) * LANES]
            force[t, v, pl.ds(j, CHUNK, stride=seg), :] = part

    def sweep(ref, which, reverse, read, store, sender, receiver, out_buf, in_buf):
        order = range(seg - 1, -1, -1) if reverse else range(seg)
        state = None
        for j in order:
            rhs = [read(v, j) for v in range(nv)]
            if state is None:
                state = rhs
            else:
                step = advance(ref, j, state)
                state = [a - b for a, b in zip(rhs, step)]
        for level in range(3):
            prev = [shifted(x, 1 << level, reverse, 0.0) for x in state]
            fresh = []
            for v in range(nv):
                terms = [maps[which, level, v, w] * prev[w] for w in range(nv)]
                fresh.append(
                    state[v] + (((terms[0] + terms[1]) + (terms[2] + terms[3])) + terms[4])
                )
            state = fresh

        has_source = place < count - 1 if reverse else place > 0
        has_target = place > 0 if reverse else place < count - 1

        @pl.when(has_source)
        def _():
            receiver.wait_recv()

        carried = [jnp.where(has_source, in_buf[v : v + 1, :], 0.0) for v in range(nv)]
        full = []
        for v in range(nv):
            terms = [maps[which, 3, v, w] * carried[w] for w in range(nv)]
            full.append(state[v] + (((terms[0] + terms[1]) + (terms[2] + terms[3])) + terms[4]))
        end = 0 if reverse else CHUNK - 1
        for v in range(nv):
            out_buf[v : v + 1, :] = full[v][end : end + 1, :]

        @pl.when(has_target)
        def _():
            sender.start()

        now = [shifted(full[v], 1, reverse, carried[v]) for v in range(nv)]
        for j in order:
            step = advance(ref, j, now)
            now = [read(v, j) - step[v] for v in range(nv)]
            for v in range(nv):
                store(v, j, now[v])

    def carry(kind, src, dst, other):
        return pltpu.make_async_remote_copy(
            src_ref=src,
            dst_ref=dst,
            send_sem=line_send.at[kind],
            recv_sem=line_recv.at[kind],
            device_id={"normal": other},
            device_id_type=MESH,
        )

    go_up = carry(0, up_out, up_in, place + 1)
    go_down = carry(1, down_out, down_in, place - 1)
    up_out[...] = jnp.zeros_like(up_out)
    down_out[...] = jnp.zeros_like(down_out)
    sweep(upper, 0, False, read_force, store_up, go_up, go_up, up_out, up_in)
    sweep(lower, 1, True, read_up, store_out, go_down, go_down, down_out, down_in)

    for t in range(tiles):
        out_ref[:, :, t * LANES : (t + 1) * LANES] = force[t]

    for copy in to_chip + to_core + onward + across:
        copy.wait_send()

    @pl.when(place < count - 1)
    def _():
        go_up.wait_send()

    @pl.when(place > 0)
    def _():
        go_down.wait_send()


def local(
    patches,
    count,
    residual_in,
    prior_iterate,
    coupling,
    line_slot,
    patch_nbr,
    edge_lines,
    upper_blocks,
    lower_blocks,
):
    nv, cells, lines = residual_in.shape
    width = edge_lines.shape[1]
    vmem = pl.BlockSpec(memory_space=pltpu.VMEM)
    hbm = pl.BlockSpec(memory_space=pl.ANY)
    seg = cells // CHUNK
    tiles = lines // LANES
    return pl.pallas_call(
        functools.partial(kernel, patches, count),
        out_shape=jax.ShapeDtypeStruct(residual_in.shape, F32),
        in_specs=[
            vmem,
            vmem,
            vmem,
            pl.BlockSpec(memory_space=pltpu.SMEM),
            vmem,
            hbm,
            hbm,
            hbm,
        ],
        out_specs=vmem,
        scratch_shapes=[
            pltpu.VMEM(residual_in.shape, F32),
            pltpu.VMEM((tiles, nv, nv, cells, LANES), F32),
            pltpu.VMEM((tiles, nv, nv, cells, LANES), F32),
            pltpu.VMEM((nv, cells, width), F32),
            pltpu.VMEM((4, nv, cells, width), F32),
            pltpu.VMEM((4 * width, lines), BF16),
            pltpu.VMEM((4 * width, lines), BF16),
            pltpu.VMEM((2, 4, nv, nv, CHUNK, lines), F32),
            pltpu.VMEM((tiles, nv, cells, LANES), F32),
            pltpu.VMEM((nv, seg, CHUNK, lines), F32),
            pltpu.VMEM((8, lines), F32),
            pltpu.VMEM((8, lines), F32),
            pltpu.VMEM((8, lines), F32),
            pltpu.VMEM((8, lines), F32),
            pltpu.SemaphoreType.DMA((3, tiles)),
            pltpu.SemaphoreType.DMA((4, nv)),
            pltpu.SemaphoreType.DMA((4, nv)),
            pltpu.SemaphoreType.DMA((2,)),
            pltpu.SemaphoreType.DMA((2,)),
        ],
        compiler_params=pltpu.CompilerParams(
            collective_id=0, has_side_effects=True, vmem_limit_bytes=40 * 2**20
        ),
    )(
        prior_iterate,
        coupling,
        line_slot,
        patch_nbr,
        edge_lines,
        residual_in,
        upper_blocks,
        lower_blocks,
    )


def solution(mesh):
    in_specs = (
        P(None, "normal", "patch"),
        P(None, "normal", "patch"),
        P(None, "patch"),
        P(None, "patch"),
        P("patch", None),
        P("patch", None),
        P(None, None, "normal", "patch"),
        P(None, None, "normal", "patch"),
    )
    body = functools.partial(local, mesh.shape["patch"], mesh.shape["normal"])
    return jax.shard_map(
        body, mesh=mesh, in_specs=in_specs, out_specs=P(None, "normal", "patch"), check_vma=False
    )
```

time: 209 us -> 33.5 us (0.16)
  the two profiles are of different devices: /device:TPU:26 before, /device:TPU:0 now
where the time goes in v1:
time: 33.5 us; the launch traced here: 33.1 us
  Pallas kernels  24.9 us (74%)
  local copies, waits for them, and re-layouts  8.21 us (25%)
    pallas_call x1, Pallas kernels, local(): pl.pallas_call(functools.partial(kernel, patches, count), out_shape=jax.S...  24.9 us
    unnamed x17, local copies, waits for them, and re-layouts  8.21 us

profile of v1, /device:TPU:0, one launch (start us, length us, event | category | flops | bytes accessed | tf_op | source)
XLA Modules:
  0.0 33.1 jit_solution(9489882351650885487)
XLA Ops:
  0.0 0.0 copy-start
  0.0 1.4 %copy-done = f32[5,5,64,256]{3,2,1,0:T(8,128)S(1)} copy-done((f32[5,5,64,256]{3,2,1,0:T(8,128)S(1)}, f32[5,5,64,256]{3,2,1,0:T(8,128)}, u32[]{:S(2)}) %copy-start) | copy-done | bytes 1638424
  1.4 0.0 copy-start.1
  1.4 1.4 %copy-done.1 = f32[5,5,64,256]{3,2,1,0:T(8,128)S(1)} copy-done((f32[5,5,64,256]{3,2,1,0:T(8,128)S(1)}, f32[5,5,64,256]{3,2,1,0:T(8,128)}, u32[]{:S(2)}) %copy-start.1) | copy-done | bytes 1638424
  2.9 0.0 copy-start.2
  2.9 1.0 %copy-done.2 = f32[5,64,256]{2,1,0:T(8,128)S(1)} copy-done((f32[5,64,256]{2,1,0:T(8,128)S(1)}, f32[5,64,256]{2,1,0:T(8,128)}, u32[]{:S(2)}) %copy-start.2) | copy-done | bytes 327704
  3.8 0.0 copy-start.3
  3.8 1.0 %copy-done.3 = f32[5,64,256]{2,1,0:T(8,128)S(1)} copy-done((f32[5,64,256]{2,1,0:T(8,128)S(1)}, f32[5,64,256]{2,1,0:T(8,128)}, u32[]{:S(2)}) %copy-start.3) | copy-done | bytes 327704
  4.8 0.0 copy-start.4
  4.8 0.7 %copy-done.4 = f32[4,256]{1,0:T(4,128)S(1)} copy-done((f32[4,256]{1,0:T(4,128)S(1)}, f32[4,256]{1,0:T(4,128)}, u32[]{:S(2)}) %copy-start.4) | copy-done | bytes 4120
  5.5 0.0 copy-start.5
  5.5 0.7 %copy-done.5 = s32[4,256]{1,0:T(4,128)S(1)} copy-done((s32[4,256]{1,0:T(4,128)S(1)}, s32[4,256]{1,0:T(4,128)}, u32[]{:S(2)}) %copy-start.5) | copy-done | bytes 4120
  6.2 0.0 copy-start.6
  6.2 0.7 %copy-done.6 = s32[1,4]{1,0:T(1,128)S(1)} copy-done((s32[1,4]{1,0:T(1,128)S(1)}, s32[1,4]{1,0:T(1,128)}, u32[]{:S(2)}) %copy-start.6) | copy-done | bytes 40
  6.8 0.0 copy-start.7
  6.8 0.7 %copy-done.7 = s32[1,128]{1,0:T(1,128)S(1)} copy-done((s32[1,128]{1,0:T(1,128)S(1)}, s32[1,128]{1,0:T(1,128)}, u32[]{:S(2)}) %copy-start.7) | copy-done | bytes 536
  7.5 24.9 %shard_map.82 = f32[5,64,256]{2,1,0:T(8,128)S(1)} custom-call(f32[5,64,256]{2,1,0:T(8,128)S(1)} %copy-done.2, f32[4,256]{1,0:T(4,128)S(1)} %copy-done.4, s32[4,256]{1,0:T(4,128)S(1)} %copy-done.5, s32[1,4]{1,0:T(1,128)S(1)} %copy-done.6, s32[1,128]{1,0:T(1,128)S(1)} %copy-done.7, f32[5,64,256]{2,1,0:T(8,128)S(1)} %copy-done.3, ...), custom_call_target="tpu_custom_call" | custom-call | tf_op jit(solution)/shard_map/pallas_call | solution.py:321
  32.4 0.7 %copy.10 = f32[5,64,256]{2,1,0:T(8,128)} copy(f32[5,64,256]{2,1,0:T(8,128)S(1)} %shard_map.82) | data formatting | bytes 655360
Async XLA Ops:
  0.0 1.4 %copy-start = (f32[5,5,64,256]{3,2,1,0:T(8,128)S(1)}, f32[5,5,64,256]{3,2,1,0:T(8,128)}, u32[]{:S(2)}) copy-start(f32[5,5,64,256]{3,2,1,0:T(8,128)} %upper_hbm.1) | copy-start | bytes 4915204
  1.4 1.4 %copy-start.1 = (f32[5,5,64,256]{3,2,1,0:T(8,128)S(1)}, f32[5,5,64,256]{3,2,1,0:T(8,128)}, u32[]{:S(2)}) copy-start(f32[5,5,64,256]{3,2,1,0:T(8,128)} %lower_hbm.1) | copy-start | bytes 4915204
  2.9 1.0 %copy-start.2 = (f32[5,64,256]{2,1,0:T(8,128)S(1)}, f32[5,64,256]{2,1,0:T(8,128)}, u32[]{:S(2)}) copy-start(f32[5,64,256]{2,1,0:T(8,128)} %prior_ref.1) | copy-start | bytes 983044
  3.8 1.0 %copy-start.3 = (f32[5,64,256]{2,1,0:T(8,128)S(1)}, f32[5,64,256]{2,1,0:T(8,128)}, u32[]{:S(2)}) copy-start(f32[5,64,256]{2,1,0:T(8,128)} %residual_hbm.1) | copy-start | bytes 983044
  4.8 0.7 %copy-start.4 = (f32[4,256]{1,0:T(4,128)S(1)}, f32[4,256]{1,0:T(4,128)}, u32[]{:S(2)}) copy-start(f32[4,256]{1,0:T(4,128)} %coupling_ref.1) | copy-start | bytes 12292
  5.5 0.7 %copy-start.5 = (s32[4,256]{1,0:T(4,128)S(1)}, s32[4,256]{1,0:T(4,128)}, u32[]{:S(2)}) copy-start(s32[4,256]{1,0:T(4,128)} %slot_ref.1) | copy-start | bytes 12292
  6.2 0.7 %copy-start.6 = (s32[1,4]{1,0:T(1,128)S(1)}, s32[1,4]{1,0:T(1,128)}, u32[]{:S(2)}) copy-start(s32[1,4]{1,0:T(1,128)} %nbr_ref.1) | copy-start | bytes 52
  6.8 0.7 %copy-start.7 = (s32[1,128]{1,0:T(1,128)S(1)}, s32[1,128]{1,0:T(1,128)}, u32[]{:S(2)}) copy-start(s32[1,128]{1,0:T(1,128)} %edge_ref.1) | copy-start | bytes 1540

commit v2 on v1

--- a/solution.py
+++ b/solution.py
@@ -26,15 +26,19 @@
 def kernel(
     patches,
     count,
-    prior_ref,
-    coupling_ref,
-    slot_ref,
+    prior_hbm,
+    coupling_hbm,
+    slot_hbm,
     nbr_ref,
-    edge_ref,
+    edge_hbm,
     residual_hbm,
     upper_hbm,
     lower_hbm,
     out_ref,
+    prior_ref,
+    coupling_ref,
+    slot_ref,
+    edge_ref,
     residual,
     upper,
     lower,
@@ -50,6 +54,7 @@
     down_out,
     down_in,
     local_sem,
+    first_sem,
     strip_send,
     strip_recv,
     line_send,
@@ -62,6 +67,19 @@
     own = lax.axis_index("patch")
     place = lax.axis_index("normal")
 
+    first = [
+        pltpu.make_async_copy(src, dst, first_sem.at[i])
+        for i, (src, dst) in enumerate(
+            (
+                (edge_hbm, edge_ref),
+                (prior_hbm, prior_ref),
+                (coupling_hbm, coupling_ref),
+                (slot_hbm, slot_ref),
+            )
+        )
+    ]
+    for load in first:
+        load.start()
     tiles = lines // LANES
     loads = [pltpu.make_async_copy(residual_hbm, residual, local_sem.at[2, 0])]
     for i, (src, dst) in enumerate(((upper_hbm, upper), (lower_hbm, lower))):
@@ -75,12 +93,12 @@
     chip = lax.rem(own // 2, 2)
     core_mate = own + 1 - 2 * core
     chip_mate = own + 2 - 4 * chip
-    ahead = lax.rem(own + 4 - 8 * chip + patches, patches)
-    behind = lax.rem(own - 4 + 8 * chip + patches, patches)
+    corner = lax.rem(chip_mate - 4 + 8 * chip + patches, patches)
+    source_corner = lax.rem(own - 4 + 8 * chip + patches, patches) + 2 - 4 * chip
     direct = 3 - 3 * chip
 
     barrier = pltpu.get_barrier_semaphore()
-    for other in (core_mate, chip_mate, behind):
+    for other in (core_mate, chip_mate, source_corner):
         pl.semaphore_signal(barrier, inc=1, device_id={"patch": other}, device_id_type=MESH)
 
     @pl.when(place > 0)
@@ -91,6 +109,8 @@
     def _():
         pl.semaphore_signal(barrier, inc=1, device_id={"normal": place + 1}, device_id_type=MESH)
 
+    for load in first:
+        load.wait()
     pick = jnp.where(
         lax.broadcasted_iota(jnp.int32, (lines, width), 0) == edge_ref[...], 1.0, 0.0
     ).astype(BF16)
@@ -117,9 +137,9 @@
 
     to_chip = [send(0, v, strip.at[v], 3 - direct, chip_mate) for v in range(nv)]
     to_core = [send(1, v, strip.at[v], 1 + core, core_mate) for v in range(nv)]
-    onward = [send(2, v, halo.at[direct, v], 3 - direct, ahead) for v in range(nv)]
+    onward = [send(2, v, strip.at[v], direct, corner) for v in range(nv)]
     across = [send(3, v, halo.at[3 - 3 * core, v], 2 - core, core_mate) for v in range(nv)]
-    for copy in to_chip + to_core:
+    for copy in to_chip + onward + to_core:
         copy.start()
 
     row = lax.broadcasted_iota(jnp.int32, (width, lines), 0)
@@ -172,7 +192,6 @@
         load.wait()
     for v in range(nv):
         to_chip[v].wait_recv()
-        onward[v].start()
         map_column(upper, 0, v, False)
         map_column(lower, 1, v, True)
 
@@ -315,24 +334,28 @@
     nv, cells, lines = residual_in.shape
     width = edge_lines.shape[1]
     vmem = pl.BlockSpec(memory_space=pltpu.VMEM)
-    hbm = pl.BlockSpec(memory_space=pl.ANY)
+    hbm = pl.BlockSpec(memory_space=pltpu.HBM)
     seg = cells // CHUNK
     tiles = lines // LANES
     return pl.pallas_call(
         functools.partial(kernel, patches, count),
         out_shape=jax.ShapeDtypeStruct(residual_in.shape, F32),
         in_specs=[
-            vmem,
-            vmem,
-            vmem,
+            hbm,
+            hbm,
+            hbm,
             pl.BlockSpec(memory_space=pltpu.SMEM),
-            vmem,
+            hbm,
             hbm,
             hbm,
             hbm,
         ],
         out_specs=vmem,
         scratch_shapes=[
+            pltpu.VMEM(prior_iterate.shape, F32),
+            pltpu.VMEM(coupling.shape, F32),
+            pltpu.VMEM(line_slot.shape, jnp.int32),
+            pltpu.VMEM(edge_lines.shape, jnp.int32),
             pltpu.VMEM(residual_in.shape, F32),
             pltpu.VMEM((tiles, nv, nv, cells, LANES), F32),
             pltpu.VMEM((tiles, nv, nv, cells, LANES), F32),
@@ -348,13 +371,14 @@
             pltpu.VMEM((8, lines), F32),
             pltpu.VMEM((8, lines), F32),
             pltpu.SemaphoreType.DMA((3, tiles)),
+            pltpu.SemaphoreType.DMA((4,)),
             pltpu.SemaphoreType.DMA((4, nv)),
             pltpu.SemaphoreType.DMA((4, nv)),
             pltpu.SemaphoreType.DMA((2,)),
             pltpu.SemaphoreType.DMA((2,)),
         ],
         compiler_params=pltpu.CompilerParams(
-            collective_id=0, has_side_effects=True, vmem_limit_bytes=40 * 2**20
+            collective_id=0, has_side_effects=True, vmem_limit_bytes=60 * 2**20
         ),
     )(
         prior_iterate,

time: 33.5 us -> 25.8 us (0.77)
  local copies, waits for them, and re-layouts: 8.21 us -> 1.72 us
  Pallas kernels: 24.9 us -> 23.6 us
    unnamed x17 -> x1, local copies, waits for them, and re-layouts: 8.21 us -> 1.72 us
    pallas_call x1, Pallas kernels: 24.9 us -> 23.6 us  [local(): pl.pallas_call(functools.partial(kernel, patches, count), out_shape=jax.S...]
where the time goes in v2:
time: 25.8 us; the launch traced here: 25.3 us
  Pallas kernels  23.6 us (91%)
  local copies, waits for them, and re-layouts  1.72 us (7%)
    pallas_call x1, Pallas kernels, local(): pl.pallas_call(functools.partial(kernel, patches, count), out_shape=jax.S...  23.6 us
    unnamed x1, local copies, waits for them, and re-layouts  1.72 us

profile of v2, /device:TPU:0, one launch (start us, length us, event | category | flops | bytes accessed | tf_op | source)
XLA Modules:
  0.0 25.3 jit_solution(1506718964677299844)
XLA Ops:
  0.0 23.6 %shard_map.82 = f32[5,64,256]{2,1,0:T(8,128)} custom-call(f32[5,64,256]{2,1,0:T(8,128)} %prior_hbm.1, f32[4,256]{1,0:T(4,128)} %coupling_hbm.1, s32[4,256]{1,0:T(4,128)} %slot_hbm.1, s32[1,4]{1,0:T(1,128)} %nbr_ref.1, s32[1,128]{1,0:T(1,128)} %edge_hbm.1, f32[5,64,256]{2,1,0:T(8,128)} %residual_hbm.1, f32[5,5,64,256]{3,2,1,0:T(8,128)} %upper_hbm.1, ...), custom_call_target="tpu_custom_call" | custom-call | tf_op jit(solution)/shard_map/pallas_call | solution.py:340
  23.6 1.7 %copy.10 = f32[5,64,256]{2,1,0:T(8,128)} copy(f32[5,64,256]{2,1,0:T(8,128)} %shard_map.82) | data formatting | bytes 655360

commit v3 on v2

--- a/solution.py
+++ b/solution.py
@@ -53,6 +53,9 @@
     up_in,
     down_out,
     down_in,
+    reply_out,
+    reply_in,
+    last_state,
     local_sem,
     first_sem,
     strip_send,
@@ -191,7 +194,6 @@
     for load in loads:
         load.wait()
     for v in range(nv):
-        to_chip[v].wait_recv()
         map_column(upper, 0, v, False)
         map_column(lower, 1, v, True)
 
@@ -208,13 +210,63 @@
                     total = total + maps[which, level, v, w] * prev[w]
                 maps[which, level + 1, v, column] = total
 
+    for level in range(3):
+        join(0, level, False)
+        join(1, level, True)
+
+    def product(which, level, v, values):
+        terms = [maps[which, level, v, w] * values[w] for w in range(nv)]
+        return ((terms[0] + terms[1]) + (terms[2] + terms[3])) + terms[4]
+
+    def scanned(which, state, reverse):
+        for level in range(3):
+            prev = [shifted(x, 1 << level, reverse, 0.0) for x in state]
+            state = [state[v] + product(which, level, v, prev) for v in range(nv)]
+        return state
+
+    def response(column):
+        start = tuple(
+            shifted(maps[0, 3, v, column], 1, False, 1.0 if v == column else 0.0)
+            for v in range(nv)
+        )
+
+        def climb(j, state):
+            state = tuple(-x for x in advance(upper, j, state))
+            for v in range(nv):
+                up_state[v, j] = state[v]
+            return state
+
+        def descend(step, state):
+            j = seg - 1 - step
+            return tuple(up_state[v, j] - x for v, x in enumerate(advance(lower, j, state)))
+
+        lax.fori_loop(0, seg, climb, start)
+        zero = tuple(jnp.zeros((CHUNK, lines), F32) for _ in range(nv))
+        end = scanned(1, list(lax.fori_loop(0, seg, descend, zero)), True)
+        for v in range(nv):
+            reply_out[v * nv + column : v * nv + column + 1, :] = end[v][0:1, :]
+
+    if count == 0:
+        reply_out[...] = jnp.zeros_like(reply_out)
+        for column in range(nv):
+            response(column)
+        reply = pltpu.make_async_remote_copy(
+            src_ref=reply_out,
+            dst_ref=reply_in,
+            send_sem=line_send.at[2],
+            recv_sem=line_recv.at[2],
+            device_id={"normal": 1 - place},
+            device_id_type=MESH,
+        )
+
+        @pl.when(place == 1)
+        def _():
+            reply.start()
+
     for v in range(nv):
+        to_chip[v].wait_recv()
         onward[v].wait_recv()
         across[v].start()
-        if v < 3:
-            join(0, v, False)
-            join(1, v, True)
-
     for v in range(nv):
         to_core[v].wait_recv()
         across[v].wait_recv()
@@ -301,8 +353,76 @@
     go_down = carry(1, down_out, down_in, place - 1)
     up_out[...] = jnp.zeros_like(up_out)
     down_out[...] = jnp.zeros_like(down_out)
-    sweep(upper, 0, False, read_force, store_up, go_up, go_up, up_out, up_in)
-    sweep(lower, 1, True, read_up, store_out, go_down, go_down, down_out, down_in)
+
+    def partial_sweep(ref, which, reverse, read):
+        state = None
+        for j in range(seg - 1, -1, -1) if reverse else range(seg):
+            rhs = [read(v, j) for v in range(nv)]
+            if state is None:
+                state = rhs
+            else:
+                step = advance(ref, j, state)
+                state = [a - b for a, b in zip(rhs, step)]
+        return scanned(which, state, reverse)
+
+    def final_sweep(ref, reverse, read, store, now):
+        for j in range(seg - 1, -1, -1) if reverse else range(seg):
+            step = advance(ref, j, now)
+            now = [read(v, j) - step[v] for v in range(nv)]
+            for v in range(nv):
+                store(v, j, now[v])
+
+    if count == 0:
+        first_up = partial_sweep(upper, 0, False, read_force)
+        for v in range(nv):
+            up_out[v : v + 1, :] = first_up[v][CHUNK - 1 :, :]
+
+        @pl.when(place == 0)
+        def _():
+            go_up.start()
+
+        start = [shifted(x, 1, False, 0.0) for x in first_up]
+        final_sweep(upper, False, read_force, store_up, start)
+        first_down = partial_sweep(lower, 1, True, read_up)
+        for v in range(nv):
+            down_out[v : v + 1, :] = first_down[v][0:1, :]
+
+        @pl.when(place == 1)
+        def _():
+            go_down.start()
+            go_up.wait_recv()
+            carried = [up_in[v : v + 1, :] for v in range(nv)]
+            full = [first_up[v] + product(0, 3, v, carried) for v in range(nv)]
+            again = [shifted(full[v], 1, False, carried[v]) for v in range(nv)]
+            final_sweep(upper, False, read_force, store_up, again)
+            second_down = partial_sweep(lower, 1, True, read_up)
+            for v in range(nv):
+                last_state[v] = shifted(second_down[v], 1, True, 0.0)
+
+        @pl.when(place == 0)
+        def _():
+            reply.wait_recv()
+            go_down.wait_recv()
+            carried = []
+            for v in range(nv):
+                total = down_in[v : v + 1, :]
+                for w in range(nv):
+                    at = v * nv + w
+                    total = total + reply_in[at : at + 1, :] * up_out[w : w + 1, :]
+                carried.append(total)
+            for v in range(nv):
+                full = first_down[v] + product(1, 3, v, carried)
+                last_state[v] = shifted(full, 1, True, carried[v])
+
+        final_sweep(lower, True, read_up, store_out, [last_state[v] for v in range(nv)])
+
+        @pl.when(place == 1)
+        def _():
+            reply.wait_send()
+
+    else:
+        sweep(upper, 0, False, read_force, store_up, go_up, go_up, up_out, up_in)
+        sweep(lower, 1, True, read_up, store_out, go_down, go_down, down_out, down_in)
 
     for t in range(tiles):
         out_ref[:, :, t * LANES : (t + 1) * LANES] = force[t]
@@ -370,12 +490,15 @@
             pltpu.VMEM((8, lines), F32),
             pltpu.VMEM((8, lines), F32),
             pltpu.VMEM((8, lines), F32),
+            pltpu.VMEM((32, lines), F32),
+            pltpu.VMEM((32, lines), F32),
+            pltpu.VMEM((nv, CHUNK, lines), F32),
             pltpu.SemaphoreType.DMA((3, tiles)),
             pltpu.SemaphoreType.DMA((4,)),
             pltpu.SemaphoreType.DMA((4, nv)),
             pltpu.SemaphoreType.DMA((4, nv)),
-            pltpu.SemaphoreType.DMA((2,)),
-            pltpu.SemaphoreType.DMA((2,)),
+            pltpu.SemaphoreType.DMA((3,)),
+            pltpu.SemaphoreType.DMA((3,)),
         ],
         compiler_params=pltpu.CompilerParams(
             collective_id=0, has_side_effects=True, vmem_limit_bytes=60 * 2**20

time: 25.8 us -> 24.1 us (0.934); the launches traced: 25.3 us -> 23.9 us
  Pallas kernels: 23.6 us -> 22.2 us
    pallas_call x1, Pallas kernels: 23.6 us -> 22.2 us  [local(): pl.pallas_call(functools.partial(kernel, patches, count), out_shape=jax.S...]
where the time goes in v3:
time: 24.1 us; the launch traced here: 23.9 us
  Pallas kernels  22.2 us (92%)
  local copies, waits for them, and re-layouts  1.72 us (7%)
    pallas_call x1, Pallas kernels, local(): pl.pallas_call(functools.partial(kernel, patches, count), out_shape=jax.S...  22.2 us
    unnamed x1, local copies, waits for them, and re-layouts  1.72 us

profile of v3, /device:TPU:0, one launch (start us, length us, event | category | flops | bytes accessed | tf_op | source)
XLA Modules:
  0.0 23.9 jit_solution(7982784378099193358)
XLA Ops:
  0.0 22.2 %shard_map.82 = f32[5,64,256]{2,1,0:T(8,128)} custom-call(f32[5,64,256]{2,1,0:T(8,128)} %prior_hbm.1, f32[4,256]{1,0:T(4,128)} %coupling_hbm.1, s32[4,256]{1,0:T(4,128)} %slot_hbm.1, s32[1,4]{1,0:T(1,128)} %nbr_ref.1, s32[1,128]{1,0:T(1,128)} %edge_hbm.1, f32[5,64,256]{2,1,0:T(8,128)} %residual_hbm.1, f32[5,5,64,256]{3,2,1,0:T(8,128)} %upper_hbm.1, ...), custom_call_target="tpu_custom_call" | custom-call | tf_op jit(solution)/shard_map/pallas_call | solution.py:460
  22.2 1.7 %copy.10 = f32[5,64,256]{2,1,0:T(8,128)} copy(f32[5,64,256]{2,1,0:T(8,128)} %shard_map.82) | data formatting | bytes 655360
